TPU v7x, 256 devices: a whole 4x4x8 slice. The times are simulated.
256 devices in a mesh: rep: 8 (over x, core), tensor: 32 (over z, y).
Axes of the slice: x: 4, y: 4, z: 8, core: 2. Of those that a mesh axis runs over, the one named last changes fastest.
Arguments:
- amplitudes: bfloat16 [2048, 8, 8192], P('tensor', None, 'rep'), may hold values from -6 to 6
- integrals: bfloat16 [32, 2048, 8192], P('tensor', None, 'rep'), as said below
- rest: bfloat16 [2048, 8, 8192], P('tensor', None, 'rep'), may hold values from -6 to 6
- occ_energy: float32 [2048], P('tensor'), may hold values from -2 to -0.4
- virt_energy: float32 [8, 8192], P(None, 'rep'), may hold values from 0.4 to 2
- sizes: int32 [8], replicated, may hold values from 4096 to 8192, as said below
- order: int32 [8], replicated, may hold values from 0 to 7, each once
Outputs:
- new_amplitudes: bfloat16 [2048, 8, 8192], P('tensor', None, 'rep')
Inputs may be any that keep to these rules, and one draw needn't show every extreme that they name: `sizes`: each is a multiple of 128, and one sector holds exactly 8192. `order`: each sector once. `integrals`: each slot's block V_k is symmetric, V_k[x, y] = V_k[y, x].
All inputs are finite; a program needn't handle non-finite values.
Results may differ from a plain program's by a relative error of at most 0.001.
Values may be sent and summed in bfloat16 or wider, within the bound.
A program may use at most 128 MiB of HBM per device.

v0:
```python
import jax
import jax.numpy as jnp
from jax import lax
from jax.sharding import PartitionSpec as P


def on_device(amplitudes, integrals, rest, occ_energy, virt_energy, sizes, order):
    groups = amplitudes.shape[1]
    width = amplitudes.shape[2]
    local_rows = amplitudes.shape[0]
    stripes = lax.axis_size("tensor") // groups
    reps = lax.axis_size("rep")
    piece_width = width // stripes
    rep_index = lax.axis_index("rep")
    column = rep_index * width + lax.broadcasted_iota(jnp.int32, (groups, width), 1)
    keep = column < sizes[:, None]
    masked = jnp.where(keep[None], amplitudes, jnp.zeros((), jnp.bfloat16))
    slotted = jnp.take(masked, order, axis=1)
    copies = jnp.repeat(slotted, stripes, axis=1)
    gathered = lax.all_to_all(copies, "tensor", split_axis=1, concat_axis=0, tiled=True)
    total_rows = gathered.shape[0]
    partial_value = jnp.einsum(
        "isy,sxy->isx", gathered, integrals, preferred_element_type=jnp.float32
    )
    folded = partial_value.reshape(total_rows, reps, piece_width)
    summed = lax.psum_scatter(folded, "rep", scatter_dimension=1, tiled=True)
    returned = lax.all_to_all(summed, "tensor", split_axis=0, concat_axis=1, tiled=True)
    ladder_slots = returned.reshape(local_rows, groups, width)
    positions = jnp.arange(groups, dtype=jnp.int32)
    inverse = jnp.sum(
        jnp.where(order[None, :] == positions[:, None], positions[None, :], 0), axis=1
    )
    ladder = jnp.take(ladder_slots, inverse, axis=1)
    denom = occ_energy[:, None, None] - virt_energy[None]
    update = (ladder + rest.astype(jnp.float32)) / denom
    return jnp.where(keep[None], update, jnp.zeros((), jnp.float32)).astype(jnp.bfloat16)


def solution(mesh):
    placed = (
        P("tensor", None, "rep"),
        P("tensor", None, "rep"),
        P("tensor", None, "rep"),
        P("tensor"),
        P(None, "rep"),
        P(),
        P(),
    )
    return jax.shard_map(
        on_device, mesh=mesh, in_specs=placed, out_specs=P("tensor", None, "rep"), check_vma=False
    )
```

profile of v0, /device:TPU:4, one launch (start us, length us, event | category | flops | bytes accessed | tf_op | source)
XLA Modules:
  0.0 322.6 jit_solution(9783883576985142940)
XLA Ops:
  6.5 0.0 reduce-scatter.2.cloned.1.call-start
  6.5 0.7 compare_select_fusion.1
  7.2 0.7 compare_and_fusion
  7.9 0.7 broadcast_compare_fusion
  8.6 2.5 copy_select_fusion
  11.1 0.6 gather_fusion
  11.7 0.2 select_bitcast_fusion
  11.8 0.5 broadcast_in_dim.75
  12.4 0.0 copy-start.3
  12.4 107.0 %all_to_all.30 = bf16[64,32,1024]{2,0,1:T(8,128)(2,1)S(1)} all-to-all(bf16[64,32,1024]{2,0,1:T(8,128)(2,1)S(1)} %bitcast.38), channel_id=1, replica_groups=mesh['rep'=8,'tensor'=32] {'tensor'}, dimensions={1} | all-to-all | bytes 8388608 | tf_op jit(solution)/shard_map/all_to_all | solution.py:20
  119.4 0.0 copy-done.3
  119.5 11.7 %fusion = f32[2048,2048]{0,1:T(8,128)} fusion(bf16[2048,1024]{1,0:T(8,128)(2,1)S(1)} %bitcast.41, bf16[1,2048,1024]{2,1,0:T(8,128)(2,1)S(1)} %copy-done.3), kind=kOutput, calls=%fused_computation.2 | convolution fusion | flops 8589934592 | bytes 25165824 | tf_op jit(solution)/shard_map/isy,sxy->isx/dot_general | solution.py:22
  131.2 16.4 %copy.28 = f32[2048,8,256]{2,0,1:T(8,128)} copy(f32[2048,8,256]{0,2,1:T(8,128)} %bitcast.39) | data formatting | bytes 33554432 | tf_op jit(solution)/shard_map/reshape | solution.py:25
  147.6 0.0 reduce-scatter.2.cloned.1.call-update
  147.6 89.3 %reduce-scatter.2.cloned.1.call-done = f32[2048,1,256]{2,0,1:T(8,128)} async-done(((f32[2048,8,256]{2,0,1:T(8,128)}), f32[2048,1,256]{2,0,1:T(8,128)}) %reduce-scatter.2.cloned.1.call-update) | async-done | bytes 2097168 | tf_op jit(solution)/shard_map/reduce_scatter | solution.py:26
  236.9 4.8 %copy.29 = f32[2048,1,256]{2,1,0:T(1,128)} copy(f32[2048,1,256]{2,0,1:T(8,128)} %reduce-scatter.2.cloned.1.call-done) | data formatting | bytes 4194304 | tf_op jit(solution)/shard_map/reduce_scatter | solution.py:26
  241.7 0.0 copy-start.4
  241.7 10.0 %all-to-all-start.1 = ((f32[2048,1,256]{2,1,0:T(1,128)}), f32[2048,1,256]{2,1,0:T(1,128)S(1)}, u32[]{:S(2)}, u32[]{:S(2)}) async-start(f32[2048,1,256]{2,1,0:T(1,128)} %copy.29), calls=%async_computation.2 | async-start | bytes 4194304 | tf_op jit(solution)/shard_map/all_to_all | solution.py:27
  251.7 0.0 copy-done.4
  251.7 0.1 select_reduce_fusion
  251.8 51.9 %all-to-all-done.1 = f32[2048,1,256]{2,1,0:T(1,128)S(1)} async-done(((f32[2048,1,256]{2,1,0:T(1,128)}), f32[2048,1,256]{2,1,0:T(1,128)S(1)}, u32[]{:S(2)}, u32[]{:S(2)}) %all-to-all-start.1) | async-done | bytes 2097184 | tf_op jit(solution)/shard_map/all_to_all | solution.py:27
  303.8 0.1 copy.34
  303.9 1.2 copy.30
  305.1 1.6 reshape.73
  306.8 4.1 %copy.31 = f32[64,8,1024]{2,0,1:T(8,128)} copy(f32[64,8,1024]{2,1,0:T(8,128)} %reshape.73) | data formatting | bytes 4194304 | tf_op jit(solution)/shard_map/reshape | solution.py:28
  310.9 0.0 copy-start
  310.9 0.0 copy-start.1
  310.9 0.0 copy-start.2
  310.9 2.4 gather_fusion.1
  313.3 0.0 copy-done
  313.3 0.0 copy-done.1
  313.3 0.0 copy-done.2
  313.3 0.9 fusion.4
  314.2 1.5 copy.33
  (5 shorter events, 0.0 us)
Async XLA Ops:
  6.5 230.3 %reduce-scatter.2.cloned.1.call-start = ((), (), s32[]{:S(2)}) async-start(), calls=%async_computation.3 | async-start | bytes 18874368 | tf_op jit(solution)/shard_map/reduce_scatter | solution.py:26
  12.4 107.1 %copy-start.3 = (bf16[1,2048,1024]{2,1,0:T(8,128)(2,1)S(1)}, bf16[1,2048,1024]{2,1,0:T(8,128)(2,1)}, u32[]{:S(2)}) copy-start(bf16[1,2048,1024]{2,1,0:T(8,128)(2,1)} %param.8) | copy-start | bytes 12582916
  241.7 10.0 %copy-start.4 = (s32[8]{0:T(128)S(1)}, s32[8]{0:T(128)}, u32[]{:S(2)}) copy-start(s32[8]{0:T(128)} %param.13) | copy-start | bytes 100
  241.7 62.1 %all-to-all-start.1 = ((f32[2048,1,256]{2,1,0:T(1,128)}), f32[2048,1,256]{2,1,0:T(1,128)S(1)}, u32[]{:S(2)}, u32[]{:S(2)}) async-start(f32[2048,1,256]{2,1,0:T(1,128)} %copy.29), calls=%async_computation.2 | async-start | bytes 4194304 | tf_op jit(solution)/shard_map/all_to_all | solution.py:27
  310.9 2.4 copy-start
  310.9 2.4 copy-start.1
  310.9 2.4 copy-start.2
Sparse Core Ops, SparseCore 0:
  147.7 89.1 reduce-scatter.1
where the time goes:
time: 324 us; the launch traced here: 323 us
  waiting for transfers between devices  141 us (44%)
  blocking collectives  107 us (33%)
  local copies, waits for them, and re-layouts  33.4 us (10%)
  between operations  13.5 us (4%)
  matrix products  11.7 us (4%)
  starting transfers between devices  9.99 us (3%)
  other arithmetic  5.71 us (2%)
    all_to_all x1, blocking collectives, on_device(): lax.all_to_all(copies, 'tensor', split_axis=1, concat_axis=0, tiled=True)  107 us
    reduce_scatter x1, waiting for transfers between devices, on_device(): summed = lax.psum_scatter(folded, 'rep', scatter_dimension=1, tiled=True)  89.3 us
    all_to_all x1, waiting for transfers between devices, on_device(): lax.all_to_all(summed, 'tensor', split_axis=0, concat_axis=1, tiled=True)  51.9 us
    reshape x1, local copies, waits for them, and re-layouts, on_device(): folded = partial_value.reshape(total_rows, reps, piece_width)  16.4 us
    dot_general x1, matrix products, on_device(): jnp.einsum('isy,sxy->isx', gathered, integrals, preferred_element_type=jn...  11.7 us
    all_to_all x1, starting transfers between devices, on_device(): lax.all_to_all(summed, 'tensor', split_axis=0, concat_axis=1, tiled=True)  9.99 us
  transfers between devices with their start and end apart: 2, of which 2 were waited for; matrix products, arithmetic and copies ran while one was open for 0% of the time, Pallas kernels for 0%

commit v1 on v0

v1 whole, which is shorter than its diff:
```python
import jax
import jax.numpy as jnp
from jax import lax
from jax.experimental import pallas as pl
from jax.experimental.pallas import tpu as pltpu
from jax.sharding import PartitionSpec as P

MESH = pl.DeviceIdType.MESH
NX, NY, NZ = 4, 4, 8
F32, BF16 = jnp.float32, jnp.bfloat16


def dot_t(a, b):
    return lax.dot_general(a, b, (((1,), (1,)), ((), ())), preferred_element_type=F32)


def kernel(
    amp_ref, int_ref, rest_ref, occ_ref, virt_ref, sizes_ref, order_ref, out_ref,
    slots, rest_slots, a_own, a_oth, v_own, v_oth, part, relay_l, relay_r, from_l, from_r, lad, upd,
    zs, zr, ys, yr, cs, cr, vs, vr, vl, xs, xr, rs, rr,
):
    rep, tensor = lax.axis_index("rep"), lax.axis_index("tensor")
    x, core = rep // 2, rep % 2
    z, y = tensor // NY, tensor % NY
    rows, width = amp_ref.shape[0] // NZ, amp_ref.shape[1]
    block = rows * NZ
    half = block // 2
    piece = width // NY

    def at_x(step):
        return lax.rem(x + step + NX, NX) * 2 + core

    def at_y(step):
        return z * NY + lax.rem(y + step + NY, NY)

    other = x * 2 + 1 - core

    def copy(src, dst, send, recv, to_rep, to_tensor):
        return pltpu.make_async_remote_copy(
            src_ref=src, dst_ref=dst, send_sem=send, recv_sem=recv,
            device_id=(to_rep, to_tensor), device_id_type=MESH,
        )

    barrier = pltpu.get_barrier_semaphore()

    def peer(dz, dy):
        return lax.rem(z + dz, NZ) * NY + lax.rem(y + dy, NY)

    for dz in range(NZ):
        for dy in range(NY):
            if dz or dy:
                pl.semaphore_signal(barrier, inc=1, device_id=(rep, peer(dz, dy)), device_id_type=MESH)
    for to in (at_x(1), at_x(-1), other):
        pl.semaphore_signal(barrier, inc=1, device_id=(to, tensor), device_id_type=MESH)

    v_local = pltpu.make_async_copy(int_ref.at[:, core], v_own, vl)
    v_local.start()

    line = lax.broadcasted_iota(jnp.int32, (rows, block), 1)
    which = lax.broadcasted_iota(jnp.int32, (rows, block), 0)
    column = rep * width + lax.broadcasted_iota(jnp.int32, (rows, width), 1)
    amp, rest = amp_ref[...], rest_ref[...]
    for k in range(NZ):
        sector = order_ref[k]
        pick = jnp.where(line == which * NZ + sector, 1.0, 0.0).astype(BF16)
        moved = jnp.dot(pick, amp, preferred_element_type=F32)
        slots[k] = jnp.where(column < sizes_ref[sector], moved, 0.0).astype(BF16)

    pl.semaphore_wait(barrier, NZ * NY - 1 + 3)

    z_copies = []
    for dz in (4, 3, 5, 2, 6, 1, 7):
        to = lax.rem(z + dz, NZ)
        c = copy(
            slots.at[to], a_own.at[0, pl.ds(pl.multiple_of(z * rows, rows), rows)],
            zs.at[dz], zr.at[dz], rep, to * NY + y,
        )
        c.start()
        z_copies.append(c)
    v_copy = copy(int_ref.at[:, 1 - core], v_oth, vs, vr, other, tensor)
    v_copy.start()
    a_own[0, pl.ds(pl.multiple_of(z * rows, rows), rows), :] = slots[z]

    for k in range(NZ):
        pick = jnp.where(line == which * NZ + order_ref[k], 1.0, 0.0).astype(BF16)
        moved = jnp.dot(pick, rest, preferred_element_type=F32)
        rest_slots[k] = moved.astype(BF16)

    upper, lower = pl.ds(0, half), pl.ds(half, half)
    y_copies = [
        copy(a_own.at[0], a_own.at[3], ys.at[0], yr.at[0], rep, at_y(1)),
        copy(a_own.at[0], a_own.at[1], ys.at[1], yr.at[1], rep, at_y(-1)),
        copy(a_own.at[3, upper], a_own.at[2, upper], ys.at[2], yr.at[2], rep, at_y(1)),
        copy(a_own.at[1, lower], a_own.at[2, lower], ys.at[3], yr.at[3], rep, at_y(-1)),
    ]
    c_copies = [copy(a_own.at[d], a_oth.at[d], cs.at[d], cr.at[d], other, tensor) for d in range(NY)]
    x_copies = [
        [
            copy(part.at[d, 2, upper], relay_l.at[d], xs.at[d, 0], xr.at[d, 0], at_x(1), tensor),
            copy(part.at[d, 2, lower], relay_r.at[d], xs.at[d, 1], xr.at[d, 1], at_x(-1), tensor),
            copy(part.at[d, 1], from_l.at[d], xs.at[d, 2], xr.at[d, 2], at_x(1), tensor),
            copy(part.at[d, 3], from_r.at[d], xs.at[d, 3], xr.at[d, 3], at_x(-1), tensor),
        ]
        for d in range(NY)
    ]
    r_copies = {}

    def compute(d, s):
        t = lax.rem(x + s, NX)

        @pl.loop(0, 2)
        def _(m):
            here = pl.ds(pl.multiple_of(m * half, half), half)
            part[d, s, here, :] = dot_t(a_own[d, here, :], v_own[t]) + dot_t(a_oth[d, here, :], v_oth[t])

    def chunk(d):
        c_copies[d].wait_recv()
        compute(d, 2)
        x_copies[d][0].start()
        x_copies[d][1].start()
        compute(d, 1)
        compute(d, 3)
        x_copies[d][0].wait_recv()
        part[d, 1, upper, :] += relay_l[d]
        x_copies[d][2].start()
        x_copies[d][1].wait_recv()
        part[d, 3, lower, :] += relay_r[d]
        x_copies[d][3].start()
        compute(d, 0)

    def finish(d):
        x_copies[d][2].wait_recv()
        x_copies[d][3].wait_recv()
        part[d, 0] += from_l[d] + from_r[d]
        for dz in range(NZ):
            to = lax.rem(z + dz, NZ)
            src = part.at[d, 0, pl.ds(pl.multiple_of(to * rows, rows), rows)]
            if dz or d:
                i = dz * NY + d
                c = copy(src, lad.at[z, y], rs.at[i], rr.at[i], rep, peer(dz, d))
                c.start()
                r_copies[i] = c
            else:
                lad[z, y] = part[d, 0, pl.ds(pl.multiple_of(z * rows, rows), rows), :]

    for c in z_copies:
        c.wait_recv()
    y_copies[0].start()
    y_copies[1].start()
    c_copies[0].start()
    v_local.wait()
    v_copy.wait_recv()
    chunk(0)
    y_copies[0].wait_recv()
    y_copies[2].start()
    c_copies[3].start()
    y_copies[1].wait_recv()
    y_copies[3].start()
    c_copies[1].start()
    chunk(3)
    finish(0)
    chunk(1)
    y_copies[2].wait_recv()
    y_copies[3].wait_recv()
    c_copies[2].start()
    finish(3)
    chunk(2)
    finish(1)
    finish(2)

    for c in r_copies.values():
        c.wait_recv()
    eye = lax.broadcasted_iota(jnp.int32, (rows, rows), 0) == lax.broadcasted_iota(jnp.int32, (rows, rows), 1)
    occ = jnp.sum(jnp.where(eye, occ_ref[...], 0.0), axis=1, keepdims=True)
    for k in range(NZ):
        sector = order_ref[k]
        virt = virt_ref[pl.ds(sector, 1), :]
        for c in range(NY):
            cols = slice(c * piece, (c + 1) * piece)
            new = (lad[k, c] + rest_slots[k, :, cols].astype(F32)) / (occ - virt[:, cols])
            new = jnp.where(column[:, cols] < sizes_ref[sector], new, 0.0)
            upd[k * rows : (k + 1) * rows, cols] = new.astype(BF16)

    wide = lax.broadcasted_iota(jnp.int32, (1, block), 1)
    lane = jnp.zeros((1, block), jnp.int32)
    for k in range(NZ):
        lane = jnp.where(wide // rows == k, (wide - k * rows) * NZ + order_ref[k], lane)
    back = jnp.where(lax.broadcasted_iota(jnp.int32, (block, block), 0) == lane, 1.0, 0.0).astype(BF16)
    out_ref[...] = jnp.dot(back, upd[...], preferred_element_type=F32).astype(BF16)

    v_copy.wait_send()
    for c in z_copies + y_copies + c_copies + sum(x_copies, []) + list(r_copies.values()):
        c.wait_send()


def on_device(amplitudes, integrals, rest, occ_energy, virt_energy, sizes, order):
    rows, groups, width = amplitudes.shape
    piece = width // NY
    block = rows * groups
    vmem, smem = pl.BlockSpec(memory_space=pltpu.VMEM), pl.BlockSpec(memory_space=pltpu.SMEM)
    dma = pltpu.SemaphoreType.DMA
    out = pl.pallas_call(
        kernel,
        out_shape=jax.ShapeDtypeStruct((block, width), BF16),
        in_specs=[vmem, pl.BlockSpec(memory_space=pl.ANY), vmem, vmem, vmem, smem, smem],
        out_specs=vmem,
        scratch_shapes=[
            pltpu.VMEM((NZ, rows, width), BF16),
            pltpu.VMEM((NZ, rows, width), BF16),
            pltpu.VMEM((NY, block, width), BF16),
            pltpu.VMEM((NY, block, width), BF16),
            pltpu.VMEM((NX, piece, width), BF16),
            pltpu.VMEM((NX, piece, width), BF16),
            pltpu.VMEM((NY, NX, block, piece), F32),
            pltpu.VMEM((NY, block // 2, piece), F32),
            pltpu.VMEM((NY, block // 2, piece), F32),
            pltpu.VMEM((NY, block, piece), F32),
            pltpu.VMEM((NY, block, piece), F32),
            pltpu.VMEM((NZ, NY, rows, piece), F32),
            pltpu.VMEM((block, width), BF16),
            dma((NZ,)), dma((NZ,)), dma((4,)), dma((4,)), dma((NY,)), dma((NY,)),
            dma(()), dma(()), dma(()),
            dma((NY, 4)), dma((NY, 4)), dma((NZ * NY,)), dma((NZ * NY,)),
        ],
        compiler_params=pltpu.CompilerParams(
            collective_id=0, has_side_effects=True, vmem_limit_bytes=56 * 2**20
        ),
        cost_estimate=pl.CostEstimate(flops=2 * 2048 * 2048 * 1024, bytes_accessed=8 << 20, transcendentals=0),
    )(
        amplitudes.reshape(block, width),
        integrals.reshape(NX, 2, piece, width),
        rest.reshape(block, width),
        occ_energy.reshape(1, rows),
        virt_energy,
        sizes,
        order,
    )
    return out.reshape(rows, groups, width)


def solution(mesh):
    placed = (
        P("tensor", None, "rep"),
        P("tensor", None, "rep"),
        P("tensor", None, "rep"),
        P("tensor"),
        P(None, "rep"),
        P(),
        P(),
    )
    return jax.shard_map(
        on_device, mesh=mesh, in_specs=placed, out_specs=P("tensor", None, "rep"), check_vma=False
    )
```

time: 324 us -> 143 us (0.44)
  Pallas kernels: 0 us -> 141 us
  waiting for transfers between devices: 141 us -> 0 us
  blocking collectives: 107 us -> 0 us
  local copies, waits for them, and re-layouts: 33.4 us -> 2.26 us
  between operations: 13.5 us -> 0.01 us
  matrix products: 11.7 us -> 0 us
  starting transfers between devices: 9.99 us -> 0 us
  other arithmetic: 5.71 us -> 0 us
    pallas_call x0 -> x1, Pallas kernels: none -> 141 us  [on_device(): pl.pallas_call(kernel, out_shape=jax.ShapeDtypeStruct((block, width), BF1...]
    all_to_all x1 -> x0, blocking collectives: 107 us -> none  [on_device(): lax.all_to_all(copies, 'tensor', split_axis=1, concat_axis=0, tiled=True)]
    reduce_scatter x1 -> x0, waiting for transfers between devices: 89.3 us -> none  [on_device(): summed = lax.psum_scatter(folded, 'rep', scatter_dimension=1, tiled=True)]
    all_to_all x1 -> x0, waiting for transfers between devices: 51.9 us -> none  [on_device(): lax.all_to_all(summed, 'tensor', split_axis=0, concat_axis=1, tiled=True)]
    reshape x3 -> x0, local copies, waits for them, and re-layouts: 22.2 us -> none  [the longest x1 16.4 us: on_device(): folded = partial_value.reshape(total_rows, reps, piece_width)]
    dot_general x1 -> x0, matrix products: 11.7 us -> none  [on_device(): jnp.einsum('isy,sxy->isx', gathered, integrals, preferred_element_type=jn...]
    all_to_all x1 -> x0, starting transfers between devices: 9.99 us -> none  [on_device(): lax.all_to_all(summed, 'tensor', split_axis=0, concat_axis=1, tiled=True)]
    reduce_scatter x1 -> x0, local copies, waits for them, and re-layouts: 4.78 us -> none  [on_device(): summed = lax.psum_scatter(folded, 'rep', scatter_dimension=1, tiled=True)]
  transfers between devices with their start and end apart: 2 -> 0, of which waited for: 2 -> 0; matrix products, arithmetic and copies ran while one was open for 0% -> 0% of each run, Pallas kernels for 0% -> 0%
where the time goes in v1:
time: 143 us
  Pallas kernels  141 us (99%)
  local copies, waits for them, and re-layouts  2.26 us (2%)
    pallas_call x1, Pallas kernels, on_device(): pl.pallas_call(kernel, out_shape=jax.ShapeDtypeStruct((block, width), BF1...  141 us

profile of v1, /device:TPU:4, one launch (start us, length us, event | category | flops | bytes accessed | tf_op | source)
XLA Modules:
  0.0 143.0 jit_solution(7491255120197434586)
XLA Ops:
  0.0 140.7 %shard_map.73 = bf16[512,1024]{1,0:T(8,128)(2,1)} custom-call(bf16[512,1024]{1,0:T(8,128)(2,1)} %bitcast.7, bf16[4,2,256,1024]{3,2,1,0:T(8,128)(2,1)} %bitcast.6, bf16[512,1024]{1,0:T(8,128)(2,1)} %bitcast.8, f32[1,64]{1,0:T(1,128)} %bitcast.9, f32[8,1024]{1,0:T(8,128)} %virt_ref.1, s32[8]{0:T(128)} %sizes_ref.1, s32[8]{0:T(128)} %order_ref.1), custom_call_target="tpu_custom_call" | custom-call | flops 8589934592 | bytes 8388608 | tf_op jit(solution)/shard_map/pallas_call | solution.py:202
  140.7 2.3 %copy.9 = bf16[64,8,1024]{2,1,0:T(8,128)(2,1)} copy(bf16[64,8,1024]{2,1,0:T(8,128)(2,1)} %bitcast.5) | data formatting | bytes 2097152

commit v2 on v0

v2 whole, which is shorter than its diff:
```python
import jax
import jax.numpy as jnp
from jax import lax
from jax.experimental import pallas as pl
from jax.experimental.pallas import tpu as pltpu
from jax.sharding import PartitionSpec as P

MESH = pl.DeviceIdType.MESH
NX, NY, NZ = 4, 4, 8
F32, BF16, I16, I32 = jnp.float32, jnp.bfloat16, jnp.int16, jnp.int32
PARTS = 2
LANES = 128
PER = 16
LN = 0.6931471805599453 / PER


def dot_t(a, b):
    return lax.dot_general(a, b, (((1,), (1,)), ((), ())), preferred_element_type=F32)


def scale_of(grouped):
    most = jnp.maximum(jnp.max(jnp.abs(grouped), axis=0), 1e-30)
    return (jnp.log(most) * (1 / LN) + (128 * PER + 1.02)).astype(I32) - 128 * PER


def fixed(grouped, code):
    return (grouped * jnp.exp((15 * PER - code).astype(F32) * LN)[None] + 32768.5).astype(I32) - 32768


def encode(ref, values):
    grouped = [v.reshape(-1, 8, LANES) for v in values]
    code = scale_of(jnp.concatenate(grouped, axis=0))
    at = 0
    for g in grouped:
        rows = g.shape[0] * 8
        ref[at : at + rows, :] = fixed(g, code).reshape(rows, LANES).astype(I16)
        at += rows
    ref[at : at + 16, :] = jnp.concatenate([code, code], axis=0).astype(I16)


def decode(ref, parts):
    rows = (ref.shape[0] - 16) // parts
    code = ref[parts * rows :, :].astype(I32)[:8]
    step = jnp.exp((code - 15 * PER).astype(F32) * LN)[None]
    out = []
    for p in range(parts):
        q = ref[p * rows : (p + 1) * rows, :].astype(I32).astype(F32)
        out.append((q.reshape(-1, 8, LANES) * step).reshape(rows, LANES))
    return out


def kernel(
    amp_ref, int_ref, rest_ref, occ_ref, virt_ref, sizes_ref, order_ref, out_ref,
    slots, rest_in, rest_slots, a_own, a_oth, v_own, v_oth, part, relay_out, relay_in, main_out, main_in, lad_out, lad_in, upd,
    zs, zr, ys, yr, cs, cr, vs, vr, vl, rl, xs, xr, rs, rr,
):
    rep, tensor = lax.axis_index("rep"), lax.axis_index("tensor")
    x, core = rep // 2, rep % 2
    z, y = tensor // NY, tensor % NY
    width = amp_ref.shape[1]
    rows = amp_ref.shape[0] // NZ
    few = rows // PARTS
    block = few * NZ
    half = block // 2
    piece = width // NY

    def at_x(step):
        return lax.rem(x + step + NX, NX) * 2 + core

    def at_y(step):
        return z * NY + lax.rem(y + step + NY, NY)

    other = x * 2 + 1 - core

    def copy(src, dst, send, recv, to_rep, to_tensor):
        return pltpu.make_async_remote_copy(
            src_ref=src, dst_ref=dst, send_sem=send, recv_sem=recv,
            device_id=(to_rep, to_tensor), device_id_type=MESH,
        )

    barrier = pltpu.get_barrier_semaphore()

    def peer(dz, dy):
        return lax.rem(z + dz, NZ) * NY + lax.rem(y + dy, NY)

    for dz in range(NZ):
        for dy in range(NY):
            if dz or dy:
                pl.semaphore_signal(barrier, inc=1, device_id=(rep, peer(dz, dy)), device_id_type=MESH)
    for to in (at_x(1), at_x(-1), other):
        pl.semaphore_signal(barrier, inc=1, device_id=(to, tensor), device_id_type=MESH)

    v_local = pltpu.make_async_copy(int_ref.at[:, core], v_own, vl)
    v_local.start()
    rest_local = pltpu.make_async_copy(rest_ref, rest_in, rl)
    rest_local.start()

    def pick(b):
        down = lax.broadcasted_iota(I32, (block, 1), 0)
        source = jnp.zeros((block, 1), I32)
        for k in range(NZ):
            source = jnp.where(down // few == k, (down - k * few + b * few) * NZ + order_ref[k], source)
        return jnp.where(lax.broadcasted_iota(I32, (block, rows * NZ), 1) == source, 1.0, 0.0).astype(BF16)

    column = rep * width + lax.broadcasted_iota(I32, (few, width), 1)

    def z_send(b):
        moved = jnp.dot(pick(b), amp_ref[...], preferred_element_type=F32)
        for k in range(NZ):
            kept = jnp.where(column < sizes_ref[order_ref[k]], moved[k * few : (k + 1) * few], 0.0)
            slots[b, k] = kept.astype(BF16)
        if b == 0:
            pl.semaphore_wait(barrier, NZ * NY - 1 + 3)
        here = pl.ds(pl.multiple_of(z * few, few), few)
        for dz in (4, 3, 5, 2, 6, 1, 7):
            to = lax.rem(z + dz, NZ)
            c = copy(slots.at[b, to], a_own.at[0, b, here], zs.at[b, dz], zr.at[b, dz], rep, to * NY + y)
            c.start()
            z_copies[b].append(c)
        a_own[0, b, here, :] = slots[b, z]

    z_copies = [[] for _ in range(PARTS)]
    for b in range(PARTS):
        z_send(b)
    v_copy = copy(int_ref.at[:, 1 - core], v_oth, vs, vr, other, tensor)
    v_copy.start()

    rest_local.wait()
    for b in range(PARTS):
        moved = jnp.dot(pick(b), rest_in[...], preferred_element_type=F32).astype(BF16)
        for k in range(NZ):
            rest_slots[b, k] = moved[k * few : (k + 1) * few]
    eye = lax.broadcasted_iota(I32, (rows, rows), 0) == lax.broadcasted_iota(I32, (rows, rows), 1)
    occ = jnp.sum(jnp.where(eye, occ_ref[...], 0.0), axis=1, keepdims=True)

    upper, lower = pl.ds(0, half), pl.ds(half, half)
    y_copies, c_copies, x_copies, r_copies = {}, {}, {}, {}
    for b in range(PARTS):
        y_copies[b] = [
            copy(a_own.at[0, b], a_own.at[3, b], ys.at[b, 0], yr.at[b, 0], rep, at_y(1)),
            copy(a_own.at[0, b], a_own.at[1, b], ys.at[b, 1], yr.at[b, 1], rep, at_y(-1)),
            copy(a_own.at[3, b, upper], a_own.at[2, b, upper], ys.at[b, 2], yr.at[b, 2], rep, at_y(1)),
            copy(a_own.at[1, b, lower], a_own.at[2, b, lower], ys.at[b, 3], yr.at[b, 3], rep, at_y(-1)),
        ]
        for d in range(NY):
            c_copies[d, b] = copy(a_own.at[d, b], a_oth.at[d, b], cs.at[d, b], cr.at[d, b], other, tensor)
            s, r = xs.at[d, b], xr.at[d, b]
            x_copies[d, b] = [
                copy(relay_out.at[d, b, 0], relay_in.at[d, b, 0], s.at[0], r.at[0], at_x(1), tensor),
                copy(relay_out.at[d, b, 1], relay_in.at[d, b, 1], s.at[1], r.at[1], at_x(-1), tensor),
                copy(main_out.at[d, b, 0], main_in.at[d, b, 0], s.at[2], r.at[2], at_x(1), tensor),
                copy(main_out.at[d, b, 1], main_in.at[d, b, 1], s.at[3], r.at[3], at_x(-1), tensor),
            ]

    left, right = slice(0, LANES), slice(LANES, 2 * LANES)

    def multiply(d, b, s):
        t = lax.rem(x + s, NX)
        part[d, b, s] = dot_t(a_own[d, b], v_own[t]) + dot_t(a_oth[d, b], v_oth[t])

    def stage1(d, b):
        c_copies[d, b].wait_recv()
        multiply(d, b, 2)
        encode(relay_out.at[d, b, 0], [part[d, b, 2, :, left]])
        x_copies[d, b][0].start()
        encode(relay_out.at[d, b, 1], [part[d, b, 2, :, right]])
        x_copies[d, b][1].start()
        for s in (1, 3, 0):
            multiply(d, b, s)

    def stage2(d, b):
        for i, s, into, rest_of in ((0, 1, left, right), (1, 3, right, left)):
            encode(main_out.at[d, b, i, 1 - i], [part[d, b, s, :, rest_of]])
            x_copies[d, b][i].wait_recv()
            [more] = decode(relay_in.at[d, b, i], 1)
            encode(main_out.at[d, b, i, i], [part[d, b, s, :, into] + more])
            x_copies[d, b][2 + i].start()

    def stage3(d, b):
        x_copies[d, b][2].wait_recv()
        x_copies[d, b][3].wait_recv()
        for h, cols in ((0, left), (1, right)):
            [one], [two] = decode(main_in.at[d, b, 0, h], 1), decode(main_in.at[d, b, 1, h], 1)
            part[d, b, 0, :, cols] = part[d, b, 0, :, cols] + one + two
        for dz in range(NZ):
            to = lax.rem(z + dz, NZ)
            here = pl.ds(pl.multiple_of(to * few, few), few)
            whole = part[d, b, 0, here, :]
            encode(lad_out.at[d, b, dz], [whole[:, left], whole[:, right]])
            if dz or d:
                c = copy(
                    lad_out.at[d, b, dz], lad_in.at[b, dz, d], rs.at[b, dz, d], rr.at[b, dz, d], rep, peer(dz, d)
                )
                c.start()
                r_copies[d, b, dz] = c

    def owner(d, b):
        c = lax.rem(y - d + NY, NY)
        cols = pl.ds(pl.multiple_of(c * piece, piece), piece)
        for dz in range(NZ):
            if dz or d:
                r_copies[d, b, dz].wait_recv()
            ladder = jnp.concatenate(decode(lad_in.at[b, dz, d] if dz or d else lad_out.at[d, b, dz], 2), axis=1)
            k = lax.rem(z - dz + NZ, NZ)
            sector = order_ref[k]
            virt = virt_ref[pl.ds(sector, 1), cols]
            new = (ladder + rest_slots[b, k, :, cols].astype(F32)) / (occ[b * few : (b + 1) * few] - virt)
            where = rep * width + c * piece + lax.broadcasted_iota(I32, (few, piece), 1)
            new = jnp.where(where < sizes_ref[sector], new, 0.0)
            upd[pl.ds(pl.multiple_of(b * block + k * few, few), few), cols] = new.astype(BF16)

    def y_send(b):
        for c in z_copies[b]:
            c.wait_recv()
        y_copies[b][0].start()
        y_copies[b][1].start()
        c_copies[0, b].start()

    def y_forward(b):
        y_copies[b][0].wait_recv()
        y_copies[b][2].start()
        c_copies[3, b].start()
        y_copies[b][1].wait_recv()
        y_copies[b][3].start()
        c_copies[1, b].start()

    def y_last(b):
        y_copies[b][2].wait_recv()
        y_copies[b][3].wait_recv()
        c_copies[2, b].start()

    y_send(0)
    v_local.wait()
    v_copy.wait_recv()
    stage1(0, 0)
    stage2(0, 0)
    y_send(1)
    y_forward(0)
    stage3(0, 0)
    stage1(0, 1)
    stage1(3, 0)
    stage2(0, 1)
    stage1(1, 0)
    stage2(3, 0)
    stage3(0, 1)
    stage2(1, 0)
    stage3(3, 0)
    y_forward(1)
    stage3(1, 0)
    stage1(3, 1)
    stage1(1, 1)
    stage2(3, 1)
    y_last(0)
    stage2(1, 1)
    stage1(2, 0)
    stage3(3, 1)
    stage2(2, 0)
    owner(0, 0)
    stage3(1, 1)
    owner(0, 1)
    y_last(1)
    stage1(2, 1)
    stage3(2, 0)
    owner(3, 0)
    stage2(2, 1)
    owner(1, 0)
    owner(3, 1)
    stage3(2, 1)
    owner(1, 1)
    owner(2, 0)
    owner(2, 1)

    wide = lax.broadcasted_iota(I32, (1, rows * NZ), 1)
    lane = jnp.zeros((1, rows * NZ), I32)
    for b in range(PARTS):
        for k in range(NZ):
            first = b * block + k * few
            lane = jnp.where(wide // few == b * NZ + k, (wide - first + b * few) * NZ + order_ref[k], lane)
    back = jnp.where(lax.broadcasted_iota(I32, (rows * NZ, rows * NZ), 0) == lane, 1.0, 0.0).astype(BF16)
    out_ref[...] = jnp.dot(back, upd[...], preferred_element_type=F32).astype(BF16)

    v_copy.wait_send()
    for group in z_copies + list(y_copies.values()) + list(x_copies.values()):
        for c in group:
            c.wait_send()
    for c in list(c_copies.values()) + list(r_copies.values()):
        c.wait_send()


def on_device(amplitudes, integrals, rest, occ_energy, virt_energy, sizes, order):
    rows, groups, width = amplitudes.shape
    piece = width // NY
    few = rows // PARTS
    block = few * groups
    coded = block + 16
    vmem, smem, where_it_is = (pl.BlockSpec(memory_space=m) for m in (pltpu.VMEM, pltpu.SMEM, pl.ANY))
    dma = pltpu.SemaphoreType.DMA
    out = pl.pallas_call(
        kernel,
        out_shape=jax.ShapeDtypeStruct((rows * groups, width), BF16),
        in_specs=[vmem, where_it_is, where_it_is, vmem, vmem, smem, smem],
        out_specs=vmem,
        scratch_shapes=[
            pltpu.VMEM((PARTS, NZ, few, width), BF16),
            pltpu.VMEM((rows * groups, width), BF16),
            pltpu.VMEM((PARTS, NZ, few, width), BF16),
            pltpu.VMEM((NY, PARTS, block, width), BF16),
            pltpu.VMEM((NY, PARTS, block, width), BF16),
            pltpu.VMEM((NX, piece, width), BF16),
            pltpu.VMEM((NX, piece, width), BF16),
            pltpu.VMEM((NY, PARTS, NX, block, piece), F32),
            pltpu.VMEM((NY, PARTS, 2, coded, LANES), I16),
            pltpu.VMEM((NY, PARTS, 2, coded, LANES), I16),
            pltpu.VMEM((NY, PARTS, 2, 2, coded, LANES), I16),
            pltpu.VMEM((NY, PARTS, 2, 2, coded, LANES), I16),
            pltpu.VMEM((NY, PARTS, NZ, 2 * few + 16, LANES), I16),
            pltpu.VMEM((PARTS, NZ, NY, 2 * few + 16, LANES), I16),
            pltpu.VMEM((rows * groups, width), BF16),
            dma((PARTS, NZ)), dma((PARTS, NZ)), dma((PARTS, 4)), dma((PARTS, 4)), dma((NY, PARTS)), dma((NY, PARTS)),
            dma(()), dma(()), dma(()), dma(()),
            dma((NY, PARTS, 4)), dma((NY, PARTS, 4)), dma((PARTS, NZ, NY)), dma((PARTS, NZ, NY)),
        ],
        compiler_params=pltpu.CompilerParams(
            collective_id=0, has_side_effects=True, vmem_limit_bytes=56 * 2**20
        ),
        cost_estimate=pl.CostEstimate(flops=2 * 2048 * 2048 * 1024, bytes_accessed=8 << 20, transcendentals=0),
    )(
        amplitudes.reshape(rows * groups, width),
        integrals.reshape(NX, 2, piece, width),
        rest.reshape(rows * groups, width),
        occ_energy.reshape(1, rows),
        virt_energy,
        sizes,
        order,
    )
    return out.reshape(rows, groups, width)


def solution(mesh):
    placed = (
        P("tensor", None, "rep"),
        P("tensor", None, "rep"),
        P("tensor", None, "rep"),
        P("tensor"),
        P(None, "rep"),
        P(),
        P(),
    )
    return jax.shard_map(
        on_device, mesh=mesh, in_specs=placed, out_specs=P("tensor", None, "rep"), check_vma=False
    )
```

time: 324 us -> 98.5 us (0.30)
  waiting for transfers between devices: 141 us -> 0 us
  blocking collectives: 107 us -> 0 us
  Pallas kernels: 0 us -> 95.2 us
  local copies, waits for them, and re-layouts: 33.4 us -> 2.26 us
  between operations: 13.5 us -> 0.01 us
  matrix products: 11.7 us -> 0 us
  starting transfers between devices: 9.99 us -> 0 us
  other arithmetic: 5.71 us -> 0 us
    all_to_all x1 -> x0, blocking collectives: 107 us -> none  [on_device(): lax.all_to_all(copies, 'tensor', split_axis=1, concat_axis=0, tiled=True)]
    pallas_call x0 -> x1, Pallas kernels: none -> 95.2 us  [on_device(): pl.pallas_call(kernel, out_shape=jax.ShapeDtypeStruct((rows * groups, wid...]
    reduce_scatter x1 -> x0, waiting for transfers between devices: 89.3 us -> none  [on_device(): summed = lax.psum_scatter(folded, 'rep', scatter_dimension=1, tiled=True)]
    all_to_all x1 -> x0, waiting for transfers between devices: 51.9 us -> none  [on_device(): lax.all_to_all(summed, 'tensor', split_axis=0, concat_axis=1, tiled=True)]
    reshape x3 -> x0, local copies, waits for them, and re-layouts: 22.2 us -> none  [the longest x1 16.4 us: on_device(): folded = partial_value.reshape(total_rows, reps, piece_width)]
    dot_general x1 -> x0, matrix products: 11.7 us -> none  [on_device(): jnp.einsum('isy,sxy->isx', gathered, integrals, preferred_element_type=jn...]
    all_to_all x1 -> x0, starting transfers between devices: 9.99 us -> none  [on_device(): lax.all_to_all(summed, 'tensor', split_axis=0, concat_axis=1, tiled=True)]
    reduce_scatter x1 -> x0, local copies, waits for them, and re-layouts: 4.78 us -> none  [on_device(): summed = lax.psum_scatter(folded, 'rep', scatter_dimension=1, tiled=True)]
  transfers between devices with their start and end apart: 2 -> 0, of which waited for: 2 -> 0; matrix products, arithmetic and copies ran while one was open for 0% -> 0% of each run, Pallas kernels for 0% -> 0%
where the time goes in v2:
time: 98.5 us; the launch traced here: 97.5 us
  Pallas kernels  95.2 us (97%)
  local copies, waits for them, and re-layouts  2.26 us (2%)
    pallas_call x1, Pallas kernels, on_device(): pl.pallas_call(kernel, out_shape=jax.ShapeDtypeStruct((rows * groups, wid...  95.2 us
    unnamed x1, local copies, waits for them, and re-layouts  2.26 us

profile of v2, /device:TPU:4, one launch (start us, length us, event | category | flops | bytes accessed | tf_op | source)
XLA Modules:
  0.0 97.5 jit_solution(18235266594699123599)
XLA Ops:
  0.0 95.2 %shard_map.73 = bf16[512,1024]{1,0:T(8,128)(2,1)} custom-call(bf16[512,1024]{1,0:T(8,128)(2,1)} %bitcast.7, bf16[4,2,256,1024]{3,2,1,0:T(8,128)(2,1)} %bitcast.6, bf16[512,1024]{1,0:T(8,128)(2,1)} %bitcast.8, f32[1,64]{1,0:T(1,128)} %bitcast.9, f32[8,1024]{1,0:T(8,128)} %virt_ref.1, s32[8]{0:T(128)} %sizes_ref.1, s32[8]{0:T(128)} %order_ref.1), custom_call_target="tpu_custom_call" | custom-call | flops 8589934592 | bytes 8388608 | tf_op jit(solution)/shard_map/pallas_call | solution.py:298
  95.3 2.3 %copy.9 = bf16[64,8,1024]{2,1,0:T(8,128)(2,1)} copy(bf16[64,8,1024]{2,1,0:T(8,128)(2,1)} %bitcast.5) | data formatting | bytes 2097152

commit v3 on v2

--- a/solution.py
+++ b/solution.py
@@ -8,7 +8,10 @@
 MESH = pl.DeviceIdType.MESH
 NX, NY, NZ = 4, 4, 8
 F32, BF16, I16, I32 = jnp.float32, jnp.bfloat16, jnp.int16, jnp.int32
-PARTS = 2
+PARTS = 4
+GROUPS = ((0, 1), (2, 3))
+ORDER = (0, 3, 1, 2)
+CHUNKS = ((0,), (1, 2), (3,))
 LANES = 128
 PER = 16
 LN = 0.6931471805599453 / PER
@@ -23,8 +26,16 @@
     return (jnp.log(most) * (1 / LN) + (128 * PER + 1.02)).astype(I32) - 128 * PER
 
 
+def scale_up(code):
+    return jnp.exp((15 * PER - code).astype(F32) * LN)
+
+
+def scale_down(code):
+    return jnp.exp((code - 15 * PER).astype(F32) * LN)
+
+
 def fixed(grouped, code):
-    return (grouped * jnp.exp((15 * PER - code).astype(F32) * LN)[None] + 32768.5).astype(I32) - 32768
+    return (grouped * scale_up(code)[None] + 32768.5).astype(I32) - 32768
 
 
 def encode(ref, values):
@@ -41,7 +52,7 @@
 def decode(ref, parts):
     rows = (ref.shape[0] - 16) // parts
     code = ref[parts * rows :, :].astype(I32)[:8]
-    step = jnp.exp((code - 15 * PER).astype(F32) * LN)[None]
+    step = scale_down(code)[None]
     out = []
     for p in range(parts):
         q = ref[p * rows : (p + 1) * rows, :].astype(I32).astype(F32)
@@ -114,10 +125,10 @@
         here = pl.ds(pl.multiple_of(z * few, few), few)
         for dz in (4, 3, 5, 2, 6, 1, 7):
             to = lax.rem(z + dz, NZ)
-            c = copy(slots.at[b, to], a_own.at[0, b, here], zs.at[b, dz], zr.at[b, dz], rep, to * NY + y)
+            c = copy(slots.at[b, to], a_own.at[b, 0, here], zs.at[b, dz], zr.at[b, dz], rep, to * NY + y)
             c.start()
             z_copies[b].append(c)
-        a_own[0, b, here, :] = slots[b, z]
+        a_own[b, 0, here, :] = slots[b, z]
 
     z_copies = [[] for _ in range(PARTS)]
     for b in range(PARTS):
@@ -136,78 +147,116 @@
     upper, lower = pl.ds(0, half), pl.ds(half, half)
     y_copies, c_copies, x_copies, r_copies = {}, {}, {}, {}
     for b in range(PARTS):
+        own = a_own.at[b]
         y_copies[b] = [
-            copy(a_own.at[0, b], a_own.at[3, b], ys.at[b, 0], yr.at[b, 0], rep, at_y(1)),
-            copy(a_own.at[0, b], a_own.at[1, b], ys.at[b, 1], yr.at[b, 1], rep, at_y(-1)),
-            copy(a_own.at[3, b, upper], a_own.at[2, b, upper], ys.at[b, 2], yr.at[b, 2], rep, at_y(1)),
-            copy(a_own.at[1, b, lower], a_own.at[2, b, lower], ys.at[b, 3], yr.at[b, 3], rep, at_y(-1)),
+            copy(own.at[0], own.at[1], ys.at[b, 0], yr.at[b, 0], rep, at_y(1)),
+            copy(own.at[0], own.at[2], ys.at[b, 1], yr.at[b, 1], rep, at_y(-1)),
+            copy(own.at[1, upper], own.at[3, upper], ys.at[b, 2], yr.at[b, 2], rep, at_y(1)),
+            copy(own.at[2, lower], own.at[3, lower], ys.at[b, 3], yr.at[b, 3], rep, at_y(-1)),
         ]
-        for d in range(NY):
-            c_copies[d, b] = copy(a_own.at[d, b], a_oth.at[d, b], cs.at[d, b], cr.at[d, b], other, tensor)
-            s, r = xs.at[d, b], xr.at[d, b]
-            x_copies[d, b] = [
-                copy(relay_out.at[d, b, 0], relay_in.at[d, b, 0], s.at[0], r.at[0], at_x(1), tensor),
-                copy(relay_out.at[d, b, 1], relay_in.at[d, b, 1], s.at[1], r.at[1], at_x(-1), tensor),
-                copy(main_out.at[d, b, 0], main_in.at[d, b, 0], s.at[2], r.at[2], at_x(1), tensor),
-                copy(main_out.at[d, b, 1], main_in.at[d, b, 1], s.at[3], r.at[3], at_x(-1), tensor),
+        for n in range(NY):
+            c_copies[n, b] = copy(own.at[n], a_oth.at[b, n], cs.at[n, b], cr.at[n, b], other, tensor)
+        for h in range(len(CHUNKS)):
+            s, r, use = xs.at[h, b], xr.at[h, b], pl.ds(0, len(CHUNKS[h]) * block + 16)
+            x_copies[h, b] = [
+                copy(relay_out.at[h, b, 0, use], relay_in.at[h, b, 0, use], s.at[0], r.at[0], at_x(1), tensor),
+                copy(relay_out.at[h, b, 1, use], relay_in.at[h, b, 1, use], s.at[1], r.at[1], at_x(-1), tensor),
+                copy(main_out.at[h, b, 0, :, use], main_in.at[h, b, 0, :, use], s.at[2], r.at[2], at_x(1), tensor),
+                copy(main_out.at[h, b, 1, :, use], main_in.at[h, b, 1, :, use], s.at[3], r.at[3], at_x(-1), tensor),
             ]
 
     left, right = slice(0, LANES), slice(LANES, 2 * LANES)
 
-    def multiply(d, b, s):
+    def span(h):
+        first, last = CHUNKS[h][0], CHUNKS[h][-1]
+        return slice(first * block, (last + 1) * block)
+
+    def multiply(h, b, s):
         t = lax.rem(x + s, NX)
-        part[d, b, s] = dot_t(a_own[d, b], v_own[t]) + dot_t(a_oth[d, b], v_oth[t])
-
-    def stage1(d, b):
-        c_copies[d, b].wait_recv()
-        multiply(d, b, 2)
-        encode(relay_out.at[d, b, 0], [part[d, b, 2, :, left]])
-        x_copies[d, b][0].start()
-        encode(relay_out.at[d, b, 1], [part[d, b, 2, :, right]])
-        x_copies[d, b][1].start()
+        here = slice(CHUNKS[h][0], CHUNKS[h][-1] + 1)
+        mine = a_own[b, here].reshape(-1, width)
+        others = a_oth[b, here].reshape(-1, width)
+        part[b, s, span(h)] = dot_t(mine, v_own[t]) + dot_t(others, v_oth[t])
+
+    def stage1(h, b):
+        for n in CHUNKS[h]:
+            c_copies[n, b].wait_recv()
+        multiply(h, b, 2)
+        encode(relay_out.at[h, b, 0], [part[b, 2, span(h), left]])
+        x_copies[h, b][0].start()
+        encode(relay_out.at[h, b, 1], [part[b, 2, span(h), right]])
+        x_copies[h, b][1].start()
         for s in (1, 3, 0):
-            multiply(d, b, s)
-
-    def stage2(d, b):
+            multiply(h, b, s)
+
+    def stage2(h, b):
+        use = pl.ds(0, len(CHUNKS[h]) * block + 16)
         for i, s, into, rest_of in ((0, 1, left, right), (1, 3, right, left)):
-            encode(main_out.at[d, b, i, 1 - i], [part[d, b, s, :, rest_of]])
-            x_copies[d, b][i].wait_recv()
-            [more] = decode(relay_in.at[d, b, i], 1)
-            encode(main_out.at[d, b, i, i], [part[d, b, s, :, into] + more])
-            x_copies[d, b][2 + i].start()
-
-    def stage3(d, b):
-        x_copies[d, b][2].wait_recv()
-        x_copies[d, b][3].wait_recv()
-        for h, cols in ((0, left), (1, right)):
-            [one], [two] = decode(main_in.at[d, b, 0, h], 1), decode(main_in.at[d, b, 1, h], 1)
-            part[d, b, 0, :, cols] = part[d, b, 0, :, cols] + one + two
-        for dz in range(NZ):
-            to = lax.rem(z + dz, NZ)
-            here = pl.ds(pl.multiple_of(to * few, few), few)
-            whole = part[d, b, 0, here, :]
-            encode(lad_out.at[d, b, dz], [whole[:, left], whole[:, right]])
-            if dz or d:
-                c = copy(
-                    lad_out.at[d, b, dz], lad_in.at[b, dz, d], rs.at[b, dz, d], rr.at[b, dz, d], rep, peer(dz, d)
-                )
-                c.start()
-                r_copies[d, b, dz] = c
-
-    def owner(d, b):
-        c = lax.rem(y - d + NY, NY)
-        cols = pl.ds(pl.multiple_of(c * piece, piece), piece)
-        for dz in range(NZ):
-            if dz or d:
-                r_copies[d, b, dz].wait_recv()
-            ladder = jnp.concatenate(decode(lad_in.at[b, dz, d] if dz or d else lad_out.at[d, b, dz], 2), axis=1)
-            k = lax.rem(z - dz + NZ, NZ)
-            sector = order_ref[k]
-            virt = virt_ref[pl.ds(sector, 1), cols]
-            new = (ladder + rest_slots[b, k, :, cols].astype(F32)) / (occ[b * few : (b + 1) * few] - virt)
+            encode(main_out.at[h, b, i, 1 - i], [part[b, s, span(h), rest_of]])
+            x_copies[h, b][i].wait_recv()
+            [more] = decode(relay_in.at[h, b, i, use], 1)
+            encode(main_out.at[h, b, i, i], [part[b, s, span(h), into] + more])
+            x_copies[h, b][2 + i].start()
+
+    def stage3(h, b):
+        use = pl.ds(0, len(CHUNKS[h]) * block + 16)
+        x_copies[h, b][2].wait_recv()
+        x_copies[h, b][3].wait_recv()
+        for i, cols in ((0, left), (1, right)):
+            [one], [two] = decode(main_in.at[h, b, 0, i, use], 1), decode(main_in.at[h, b, 1, i, use], 1)
+            part[b, 0, span(h), cols] = part[b, 0, span(h), cols] + one + two
+
+    def give_back(h, g):
+        parts = len(GROUPS[g])
+        tall = pl.ds(0, 2 * parts * few + 16)
+        for n in CHUNKS[h]:
+            d = ORDER[n]
+            here = slice(n * block, (n + 1) * block)
+            values = [
+                part[b, 0, here, cols].reshape(NZ, few // 8, 8, LANES) for b in GROUPS[g] for cols in (left, right)
+            ]
+            code = scale_of(jnp.concatenate([jnp.swapaxes(v, 0, 1) for v in values], axis=0))
+            up = scale_up(code)[:, None]
+            for i, v in enumerate(values):
+                q = ((v * up + 32768.5).astype(I32) - 32768).reshape(NZ, few, LANES)
+                lad_out[g, d, :, i * few : (i + 1) * few, :] = q.astype(I16)
+            lad_out[g, d, :, 2 * parts * few : 2 * parts * few + 16, :] = jnp.concatenate([code, code], axis=1).astype(I16)
+            for dz in range(NZ):
+                to = lax.rem(z + dz, NZ)
+                if dz or d:
+                    c = copy(
+                        lad_out.at[g, d, to, tall], lad_in.at[g, d, z, tall],
+                        rs.at[g, dz, d], rr.at[g, dz, d], rep, peer(dz, d)
+                    )
+                    c.start()
+                    r_copies[g, dz, d] = c
+                else:
+                    lad_in[g, d, pl.ds(z, 1)] = lad_out[g, d, pl.ds(z, 1)]
+
+    def owner(h, g):
+        parts = len(GROUPS[g])
+        for n in CHUNKS[h]:
+            d = ORDER[n]
+            c = lax.rem(y - d + NY, NY)
+            cols = pl.ds(pl.multiple_of(c * piece, piece), piece)
             where = rep * width + c * piece + lax.broadcasted_iota(I32, (few, piece), 1)
-            new = jnp.where(where < sizes_ref[sector], new, 0.0)
-            upd[pl.ds(pl.multiple_of(b * block + k * few, few), few), cols] = new.astype(BF16)
+            for dz in range(NZ):
+                if dz or d:
+                    r_copies[g, dz, d].wait_recv()
+            code = lad_in[g, d, :, 2 * parts * few : 2 * parts * few + 16, :].astype(I32)[:, :8]
+            step = scale_down(code)[:, None]
+            for p, b in enumerate(GROUPS[g]):
+                ladder = []
+                for i in (2 * p, 2 * p + 1):
+                    q = lad_in[g, d, :, i * few : (i + 1) * few, :].astype(I32).astype(F32)
+                    ladder.append((q.reshape(NZ, few // 8, 8, LANES) * step).reshape(NZ, few, LANES))
+                for k in range(NZ):
+                    total = jnp.concatenate([ladder[0][k], ladder[1][k]], axis=1) + rest_slots[b, k, :, cols].astype(F32)
+                    sector = order_ref[k]
+                    virt = virt_ref[pl.ds(sector, 1), cols]
+                    new = total / (occ[b * few : (b + 1) * few] - virt)
+                    new = jnp.where(where < sizes_ref[sector], new, 0.0)
+                    upd[b * block + k * few : b * block + (k + 1) * few, cols] = new.astype(BF16)
 
     def y_send(b):
         for c in z_copies[b]:
@@ -219,55 +268,77 @@
     def y_forward(b):
         y_copies[b][0].wait_recv()
         y_copies[b][2].start()
-        c_copies[3, b].start()
+        c_copies[1, b].start()
         y_copies[b][1].wait_recv()
         y_copies[b][3].start()
-        c_copies[1, b].start()
+        c_copies[2, b].start()
 
     def y_last(b):
         y_copies[b][2].wait_recv()
         y_copies[b][3].wait_recv()
-        c_copies[2, b].start()
+        c_copies[3, b].start()
 
     y_send(0)
     v_local.wait()
     v_copy.wait_recv()
     stage1(0, 0)
-    stage2(0, 0)
     y_send(1)
     y_forward(0)
+    stage2(0, 0)
+    stage1(0, 1)
+    y_send(2)
+    stage1(1, 0)
+    stage2(0, 1)
+    y_forward(1)
+    stage1(0, 2)
+    stage2(1, 0)
+    y_send(3)
+    stage1(1, 1)
+    y_last(0)
+    stage2(0, 2)
+    stage1(0, 3)
+    y_forward(2)
+    stage1(2, 0)
+    stage2(1, 1)
+    y_last(1)
     stage3(0, 0)
-    stage1(0, 1)
-    stage1(3, 0)
-    stage2(0, 1)
-    stage1(1, 0)
-    stage2(3, 0)
     stage3(0, 1)
-    stage2(1, 0)
-    stage3(3, 0)
-    y_forward(1)
+    stage2(0, 3)
     stage3(1, 0)
-    stage1(3, 1)
-    stage1(1, 1)
-    stage2(3, 1)
-    y_last(0)
-    stage2(1, 1)
-    stage1(2, 0)
-    stage3(3, 1)
+    give_back(0, 0)
+    stage1(2, 1)
     stage2(2, 0)
+    stage3(1, 1)
+    give_back(1, 0)
+    y_forward(3)
+    stage1(1, 2)
+    stage2(2, 1)
+    stage1(1, 3)
+    stage2(1, 2)
+    stage3(2, 0)
+    stage3(2, 1)
+    y_last(2)
+    give_back(2, 0)
+    stage3(0, 2)
+    stage2(1, 3)
     owner(0, 0)
-    stage3(1, 1)
+    stage3(0, 3)
+    y_last(3)
+    give_back(0, 1)
+    stage1(2, 2)
+    stage3(1, 2)
+    owner(1, 0)
+    stage1(2, 3)
+    stage3(1, 3)
+    give_back(1, 1)
+    stage2(2, 2)
+    stage2(2, 3)
+    owner(2, 0)
+    stage3(2, 2)
+    stage3(2, 3)
+    give_back(2, 1)
+    owner(1, 1)
     owner(0, 1)
-    y_last(1)
-    stage1(2, 1)
-    stage3(2, 0)
-    owner(3, 0)
-    stage2(2, 1)
-    owner(1, 0)
-    owner(3, 1)
-    stage3(2, 1)
-    owner(1, 1)
-    owner(2, 0)
     owner(2, 1)
 
     wide = lax.broadcasted_iota(I32, (1, rows * NZ), 1)
@@ -292,7 +363,8 @@
     piece = width // NY
     few = rows // PARTS
     block = few * groups
-    coded = block + 16
+    coded = 2 * block + 16
+    back = 2 * few * max(len(g) for g in GROUPS) + 16
     vmem, smem, where_it_is = (pl.BlockSpec(memory_space=m) for m in (pltpu.VMEM, pltpu.SMEM, pl.ANY))
     dma = pltpu.SemaphoreType.DMA
     out = pl.pallas_call(
@@ -304,21 +376,21 @@
             pltpu.VMEM((PARTS, NZ, few, width), BF16),
             pltpu.VMEM((rows * groups, width), BF16),
             pltpu.VMEM((PARTS, NZ, few, width), BF16),
-            pltpu.VMEM((NY, PARTS, block, width), BF16),
-            pltpu.VMEM((NY, PARTS, block, width), BF16),
+            pltpu.VMEM((PARTS, NY, block, width), BF16),
+            pltpu.VMEM((PARTS, NY, block, width), BF16),
             pltpu.VMEM((NX, piece, width), BF16),
             pltpu.VMEM((NX, piece, width), BF16),
-            pltpu.VMEM((NY, PARTS, NX, block, piece), F32),
-            pltpu.VMEM((NY, PARTS, 2, coded, LANES), I16),
-            pltpu.VMEM((NY, PARTS, 2, coded, LANES), I16),
-            pltpu.VMEM((NY, PARTS, 2, 2, coded, LANES), I16),
-            pltpu.VMEM((NY, PARTS, 2, 2, coded, LANES), I16),
-            pltpu.VMEM((NY, PARTS, NZ, 2 * few + 16, LANES), I16),
-            pltpu.VMEM((PARTS, NZ, NY, 2 * few + 16, LANES), I16),
+            pltpu.VMEM((PARTS, NX, NY * block, piece), F32),
+            pltpu.VMEM((len(CHUNKS), PARTS, 2, coded, LANES), I16),
+            pltpu.VMEM((len(CHUNKS), PARTS, 2, coded, LANES), I16),
+            pltpu.VMEM((len(CHUNKS), PARTS, 2, 2, coded, LANES), I16),
+            pltpu.VMEM((len(CHUNKS), PARTS, 2, 2, coded, LANES), I16),
+            pltpu.VMEM((len(GROUPS), NY, NZ, back, LANES), I16),
+            pltpu.VMEM((len(GROUPS), NY, NZ, back, LANES), I16),
             pltpu.VMEM((rows * groups, width), BF16),
             dma((PARTS, NZ)), dma((PARTS, NZ)), dma((PARTS, 4)), dma((PARTS, 4)), dma((NY, PARTS)), dma((NY, PARTS)),
             dma(()), dma(()), dma(()), dma(()),
-            dma((NY, PARTS, 4)), dma((NY, PARTS, 4)), dma((PARTS, NZ, NY)), dma((PARTS, NZ, NY)),
+            dma((len(CHUNKS), PARTS, 4)), dma((len(CHUNKS), PARTS, 4)), dma((len(GROUPS), NZ, NY)), dma((len(GROUPS), NZ, NY)),
         ],
         compiler_params=pltpu.CompilerParams(
             collective_id=0, has_side_effects=True, vmem_limit_bytes=56 * 2**20

time: 98.5 us -> 87.7 us (0.89)
  Pallas kernels: 95.2 us -> 84.7 us
    pallas_call x1, Pallas kernels: 95.2 us -> 84.7 us  [on_device(): pl.pallas_call(kernel, out_shape=jax.ShapeDtypeStruct((rows * groups, wid...]
where the time goes in v3:
time: 87.7 us; the launch traced here: 86.9 us
  Pallas kernels  84.7 us (97%)
  local copies, waits for them, and re-layouts  2.26 us (3%)
    pallas_call x1, Pallas kernels, on_device(): pl.pallas_call(kernel, out_shape=jax.ShapeDtypeStruct((rows * groups, wid...  84.7 us
    unnamed x1, local copies, waits for them, and re-layouts  2.26 us

profile of v3, /device:TPU:4, one launch (start us, length us, event | category | flops | bytes accessed | tf_op | source)
XLA Modules:
  0.0 86.9 jit_solution(9817359967347622862)
XLA Ops:
  0.0 84.7 %shard_map.73 = bf16[512,1024]{1,0:T(8,128)(2,1)} custom-call(bf16[512,1024]{1,0:T(8,128)(2,1)} %bitcast.7, bf16[4,2,256,1024]{3,2,1,0:T(8,128)(2,1)} %bitcast.6, bf16[512,1024]{1,0:T(8,128)(2,1)} %bitcast.8, f32[1,64]{1,0:T(1,128)} %bitcast.9, f32[8,1024]{1,0:T(8,128)} %virt_ref.1, s32[8]{0:T(128)} %sizes_ref.1, s32[8]{0:T(128)} %order_ref.1), custom_call_target="tpu_custom_call" | custom-call | flops 8589934592 | bytes 8388608 | tf_op jit(solution)/shard_map/pallas_call | solution.py:370
  84.7 2.3 %copy.9 = bf16[64,8,1024]{2,1,0:T(8,128)(2,1)} copy(bf16[64,8,1024]{2,1,0:T(8,128)(2,1)} %bitcast.5) | data formatting | bytes 2097152

commit v4 on v3

--- a/solution.py
+++ b/solution.py
@@ -292,53 +292,53 @@
     y_forward(1)
     stage1(0, 2)
     stage2(1, 0)
+    y_last(0)
+    stage3(0, 0)
     y_send(3)
+    stage3(0, 1)
     stage1(1, 1)
-    y_last(0)
+    stage1(2, 0)
     stage2(0, 2)
+    y_forward(2)
     stage1(0, 3)
-    y_forward(2)
-    stage1(2, 0)
     stage2(1, 1)
+    stage3(1, 0)
     y_last(1)
-    stage3(0, 0)
-    stage3(0, 1)
+    give_back(0, 0)
+    stage1(1, 2)
     stage2(0, 3)
-    stage3(1, 0)
-    give_back(0, 0)
     stage1(2, 1)
-    stage2(2, 0)
     stage3(1, 1)
     give_back(1, 0)
     y_forward(3)
-    stage1(1, 2)
+    stage2(1, 2)
+    owner(0, 0)
+    stage3(0, 2)
+    stage1(1, 3)
     stage2(2, 1)
-    stage1(1, 3)
-    stage2(1, 2)
+    y_last(2)
+    stage2(2, 0)
+    stage3(0, 3)
+    give_back(0, 1)
+    stage2(1, 3)
+    y_last(3)
+    stage1(2, 2)
+    stage3(2, 1)
     stage3(2, 0)
-    stage3(2, 1)
-    y_last(2)
     give_back(2, 0)
-    stage3(0, 2)
-    stage2(1, 3)
-    owner(0, 0)
-    stage3(0, 3)
-    y_last(3)
-    give_back(0, 1)
-    stage1(2, 2)
+    stage1(2, 3)
     stage3(1, 2)
-    owner(1, 0)
-    stage1(2, 3)
     stage3(1, 3)
     give_back(1, 1)
+    stage2(2, 3)
     stage2(2, 2)
-    stage2(2, 3)
+    stage3(2, 3)
+    stage3(2, 2)
+    give_back(2, 1)
+    owner(1, 0)
+    owner(0, 1)
+    owner(1, 1)
     owner(2, 0)
-    stage3(2, 2)
-    stage3(2, 3)
-    give_back(2, 1)
-    owner(1, 1)
-    owner(0, 1)
     owner(2, 1)
 
     wide = lax.broadcasted_iota(I32, (1, rows * NZ), 1)

time: 87.7 us -> 88 us (level)
  no operation moved by 1% of the time
where the time goes in v4:
time: 88 us; the launch traced here: 87 us
  Pallas kernels  84.8 us (96%)
  local copies, waits for them, and re-layouts  2.26 us (3%)
    pallas_call x1, Pallas kernels, on_device(): pl.pallas_call(kernel, out_shape=jax.ShapeDtypeStruct((rows * groups, wid...  84.8 us
    unnamed x1, local copies, waits for them, and re-layouts  2.26 us

profile of v4, /device:TPU:4, one launch (start us, length us, event | category | flops | bytes accessed | tf_op | source)
XLA Modules:
  0.0 87.0 jit_solution(10842919718197736922)
XLA Ops:
  0.0 84.8 %shard_map.73 = bf16[512,1024]{1,0:T(8,128)(2,1)} custom-call(bf16[512,1024]{1,0:T(8,128)(2,1)} %bitcast.7, bf16[4,2,256,1024]{3,2,1,0:T(8,128)(2,1)} %bitcast.6, bf16[512,1024]{1,0:T(8,128)(2,1)} %bitcast.8, f32[1,64]{1,0:T(1,128)} %bitcast.9, f32[8,1024]{1,0:T(8,128)} %virt_ref.1, s32[8]{0:T(128)} %sizes_ref.1, s32[8]{0:T(128)} %order_ref.1), custom_call_target="tpu_custom_call" | custom-call | flops 8589934592 | bytes 8388608 | tf_op jit(solution)/shard_map/pallas_call | solution.py:370
  84.8 2.3 %copy.9 = bf16[64,8,1024]{2,1,0:T(8,128)(2,1)} copy(bf16[64,8,1024]{2,1,0:T(8,128)(2,1)} %bitcast.5) | data formatting | bytes 2097152
